TPU v7x, 32 devices: a whole 2x2x4 slice. The times are simulated.
32 devices in a mesh: aux: 4 (over y, x), orb: 8 (over z, core).
Axes of the slice: x: 2, y: 2, z: 4, core: 2. Of those that a mesh axis runs over, the one named last changes fastest.
Arguments:
- integrals: bfloat16 [16, 15360, 2048], P(None, 'aux', 'orb'), may hold values from -6 to 6
- coeffs: bfloat16 [2048, 2048], P('orb'), may hold values from -1 to 1
- domains: int32 [16], replicated, may hold values from 0 to 15
- eps_occ: float32 [16], replicated, may hold values from -1.5 to -0.3
- eps_vir: float32 [2048], replicated, may hold values from 0.1 to 2.5
- pair_mask: int32 [16, 16], P('aux', 'orb'), may hold values 0 or 1
Outputs:
- amplitudes: bfloat16 [16, 128, 16, 128], P('aux', None, 'orb')
- energies: float32 [16, 16], P('aux', 'orb')
Inputs may be any that keep to these rules, and one draw needn't show every extreme that they name: `domains`: each entry names one of the 16 virtual blocks.
All inputs are finite; a program needn't handle non-finite values. No bound on the sum of `pair_mask` on one device may be relied on, other than what follows from the above.
Results may differ from a plain program's by a relative error of at most 0.019.
Values may be sent and summed in bfloat16 or wider, within the bound.
A program may use at most 128 MiB of HBM per device.

v0:
```python
import jax
import jax.numpy as jnp
from jax import lax
from jax.sharding import PartitionSpec as P

NAUX = 15360
BS = 128


def shards(integrals, coeffs, domains, eps_occ, eps_vir, pair_mask):
    occupied, aux_rows, ao_local = integrals.shape
    vir_blocks = coeffs.shape[1] // BS
    selector = domains[:, None] == jnp.arange(vir_blocks, dtype=jnp.int32)[None, :]
    chosen = jnp.einsum(
        "in,mnb->imb",
        selector.astype(jnp.bfloat16),
        coeffs.reshape(ao_local, vir_blocks, BS),
        preferred_element_type=jnp.float32,
    ).astype(jnp.bfloat16)
    orb_index = lax.axis_index("orb")
    own_count = occupied // lax.axis_size("orb")
    own_blocks = lax.psum_scatter(
        jnp.einsum("ipm,imb->ipb", integrals, chosen, preferred_element_type=jnp.float32).astype(
            jnp.bfloat16
        ),
        "orb",
        scatter_dimension=0,
        tiled=True,
    )
    all_blocks = lax.all_gather(own_blocks, "orb", axis=0, tiled=True)
    aux_index = lax.axis_index("aux")
    row_count = occupied // lax.axis_size("aux")
    totals = lax.psum_scatter(
        jnp.einsum(
            "jpb,ipa->jbia", all_blocks, own_blocks, preferred_element_type=jnp.float32
        ).astype(jnp.bfloat16),
        "aux",
        scatter_dimension=0,
        tiled=True,
    ).astype(jnp.float32)
    pair_ints = totals * (1.0 / jnp.sqrt(jnp.float32(NAUX)))
    vir_energy = jnp.dot(
        selector.astype(jnp.float32),
        eps_vir.reshape(vir_blocks, BS),
        precision=lax.Precision.HIGHEST,
    )
    vir_rows = lax.dynamic_slice_in_dim(vir_energy, aux_index * row_count, row_count, 0)
    vir_cols = lax.dynamic_slice_in_dim(vir_energy, orb_index * own_count, own_count, 0)
    occ_rows = lax.dynamic_slice_in_dim(eps_occ, aux_index * row_count, row_count, 0)
    occ_cols = lax.dynamic_slice_in_dim(eps_occ, orb_index * own_count, own_count, 0)
    denominator = (
        vir_rows[:, :, None, None]
        + vir_cols[None, None, :, :]
        - occ_rows[:, None, None, None]
        - occ_cols[None, None, :, None]
    )
    screen = pair_mask.astype(jnp.float32)
    amplitudes = screen[:, None, :, None] * pair_ints / denominator
    energies = -jnp.sum(pair_ints * amplitudes, axis=(1, 3)) / float(BS * BS)
    return (amplitudes.astype(jnp.bfloat16), energies)


def solution(mesh):
    return jax.shard_map(
        shards,
        mesh=mesh,
        in_specs=(P(None, "aux", "orb"), P("orb", None), P(), P(), P(), P("aux", "orb")),
        out_specs=(P("aux", None, "orb", None), P("aux", "orb")),
        check_vma=False,
    )
```

profile of v0, /device:TPU:23, one launch (start us, length us, event | category | flops | bytes accessed | tf_op | source)
XLA Modules:
  0.0 378.9 jit_solution(7079685104841068386)
XLA Ops:
  7.2 0.0 copy-start
  7.2 0.0 reduce-scatter.3.cloned.1.call-start
  7.2 1.4 copy.23
  8.7 1.1 fusion.16
  9.8 0.8 copy.17
  10.6 19.3 %convert_bitcast_fusion = bf16[16,3840,128]{1,2,0:T(8,128)(2,1)} fusion(bf16[16,3840,256]{2,1,0:T(8,128)(2,1)} %param.6, bf16[16,256,128]{1,2,0:T(8,128)(2,1)S(1)} %copy.17), kind=kOutput, calls=%fused_computation.2 | convolution fusion | flops 4034396160 | bytes 48234496 | tf_op jit(solution)/shard_map/ipm,imb->ipb/dot_general | solution.py:23
  29.9 0.0 reduce-scatter.3.cloned.1.call-update
  29.9 0.0 all-gather.2.cloned.1.call-start
  30.0 158.4 %reduce-scatter.3.cloned.1.call-done = bf16[2,3840,128]{1,2,0:T(8,128)(2,1)} async-done(((bf16[16,3840,128]{1,2,0:T(8,128)(2,1)}), bf16[2,3840,128]{1,2,0:T(8,128)(2,1)}) %reduce-scatter.3.cloned.1.call-update) | async-done | bytes 1966096 | tf_op jit(solution)/shard_map/reduce_scatter | solution.py:22
  188.4 4.0 %copy.11 = bf16[2,3840,128]{2,1,0:T(8,128)(2,1)} copy(bf16[2,3840,128]{1,2,0:T(8,128)(2,1)} %reduce-scatter.3.cloned.1.call-done) | data formatting | bytes 3932160 | tf_op jit(solution)/shard_map/reduce_scatter | solution.py:22
  192.3 0.0 copy-start.3
  192.3 0.0 copy-start.1
  192.3 0.0 copy-start.2
  192.3 0.0 all-gather.2.cloned.1.call-update
  192.4 0.0 reduce-scatter.5.cloned.1.call-start
  192.4 141.3 %all-gather.2.cloned.1.call-done = bf16[16,3840,128]{2,1,0:T(8,128)(2,1)} async-done(((bf16[2,3840,128]{2,1,0:T(8,128)(2,1)}), bf16[16,3840,128]{2,1,0:T(8,128)(2,1)}) %all-gather.2.cloned.1.call-update) | async-done | bytes 15728656 | tf_op jit(solution)/shard_map/all_gather | solution.py:30
  333.7 9.1 %fusion.3 = bf16[16,128,2,128]{3,1,2,0:T(8,128)(2,1)} fusion(bf16[2,3840,128]{1,2,0:T(8,128)(2,1)} %reduce-scatter.3.cloned.1.call-done, bf16[16,3840,128]{2,1,0:T(8,128)(2,1)} %all-gather.2.cloned.1.call-done), kind=kOutput, calls=%fused_computation.4 | convolution fusion | flops 4027056128 | bytes 18743296 | tf_op jit(solution)/shard_map/jpb,ipa->jbia/dot_general | solution.py:34
  342.8 0.0 reduce-scatter.5.cloned.1.call-update
  342.8 0.0 copy-done.3
  342.8 0.1 dynamic_slice.15
  342.9 0.1 dynamic_slice.14
  343.0 0.0 copy-done.1
  343.0 0.1 copy.14
  343.1 0.0 copy-done
  343.1 0.0 copy-done.2
  343.1 0.2 fusion.13
  343.3 26.0 %reduce-scatter.5.cloned.1.call-done = bf16[4,128,2,128]{3,1,2,0:T(8,128)(2,1)} async-done(((bf16[16,128,2,128]{3,1,2,0:T(8,128)(2,1)}), bf16[4,128,2,128]{3,1,2,0:T(8,128)(2,1)}) %reduce-scatter.5.cloned.1.call-update) | async-done | bytes 262160 | tf_op jit(solution)/shard_map/reduce_scatter | solution.py:33
  369.3 1.4 fusion.11
  370.7 1.0 copy.15
  371.7 0.7 copy.16
  (4 shorter events, 0.0 us)
Async XLA Ops:
  7.2 335.9 %copy-start = (f32[2048]{0:T(1024)S(1)}, f32[2048]{0:T(1024)}, u32[]{:S(2)}) copy-start(f32[2048]{0:T(1024)} %param.10) | copy-start | bytes 24580
  7.2 181.2 %reduce-scatter.3.cloned.1.call-start = ((), (), s32[]{:S(2)}) async-start(), calls=%async_computation.2 | async-start | bytes 17694720 | tf_op jit(solution)/shard_map/reduce_scatter | solution.py:22
  29.9 303.8 %all-gather.2.cloned.1.call-start = ((), (), s32[]{:S(2)}) async-start(), calls=%async_computation.3 | async-start | bytes 17694720 | tf_op jit(solution)/shard_map/all_gather | solution.py:30
  192.3 150.5 %copy-start.3 = (f32[16]{0:T(128)S(1)}, f32[16]{0:T(128)}, u32[]{:S(2)}) copy-start(f32[16]{0:T(128)} %param.9) | copy-start | bytes 196
  192.3 150.6 %copy-start.1 = (s32[4,2]{0,1:T(2,128)S(1)}, s32[4,2]{0,1:T(2,128)}, u32[]{:S(2)}) copy-start(s32[4,2]{0,1:T(2,128)} %param.11) | copy-start | bytes 100
  192.3 150.8 %copy-start.2 = (s32[16]{0:T(128)S(1)}, s32[16]{0:T(128)}, u32[]{:S(2)}) copy-start(s32[16]{0:T(128)} %param.8) | copy-start | bytes 196
  192.4 177.0 %reduce-scatter.5.cloned.1.call-start = ((), (), s32[]{:S(2)}) async-start(), calls=%async_computation.4 | async-start | bytes 1310720 | tf_op jit(solution)/shard_map/reduce_scatter | solution.py:33
Sparse Core Ops, SparseCore 0:
  30.0 158.2 reduce-scatter.2
  192.5 141.1 all-gather.1
  342.9 26.3 reduce-scatter.4
where the time goes:
time: 382 us; the launch traced here: 379 us
  waiting for transfers between devices  326 us (85%)
  matrix products  29.7 us (8%)
  between operations  13.8 us (4%)
  local copies, waits for them, and re-layouts  8.13 us (2%)
    reduce_scatter x1, waiting for transfers between devices, shards(): lax.psum_scatter(jnp.einsum('ipm,imb->ipb', integrals, chosen, preferred_...  158 us
    all_gather x1, waiting for transfers between devices, shards(): all_blocks = lax.all_gather(own_blocks, 'orb', axis=0, tiled=True)  141 us
    reduce_scatter x1, waiting for transfers between devices, shards(): lax.psum_scatter(jnp.einsum('jpb,ipa->jbia', all_blocks, own_blocks, pref...  26 us
    dot_general x1, matrix products, shards(): jnp.einsum('ipm,imb->ipb', integrals, chosen, preferred_element_type=jnp....  19.3 us
    dot_general x1, matrix products, shards(): jnp.einsum('jpb,ipa->jbia', all_blocks, own_blocks, preferred_element_typ...  9.1 us
  transfers between devices with their start and end apart: 3, of which 3 were waited for; matrix products, arithmetic and copies ran while one was open for 0% of the time, Pallas kernels for 0%

commit v1 on v0

v1 whole, which is shorter than its diff:
```python
import functools

import jax
import jax.numpy as jnp
from jax import lax
from jax.experimental import pallas as pl
from jax.experimental.pallas import tpu as pltpu
from jax.sharding import PartitionSpec as P

NAUX = 15360
BS = 128
GROUP = 2 * BS
CHUNK_ROWS = 240
LEAD = 4
SLOTS = 4
IN_FLIGHT = 4
MESH = pl.DeviceIdType.MESH


def exchange(
    dims,
    coef_ref, x_ref, total_ref,
    xo, xp, zin, pin, psend, bt, gsend, grecv, gz, gfin,
    xo_sem, xp_sem, ps_sem, pr_sem, zs_sem, zr_sem, gs_sem, gr_sem, fs_sem, fr_sem,
):
    n_aux, n_orb, groups, per_group, row_groups = dims
    chips = n_orb // 2
    half = per_group * CHUNK_ROWS
    chunks = groups * per_group
    aux = lax.axis_index("aux")
    orb = lax.axis_index("orb")
    core = lax.rem(orb, 2)
    chip = orb // 2
    peer = chip * 2 + 1 - core
    stage = jnp.where(core == 0, chip, chips - 1 - chip)
    following = jnp.where(core == 0, lax.rem(orb + 2, n_orb), lax.rem(orb + n_orb - 2, n_orb))
    last = stage == chips - 1

    barrier = pltpu.get_barrier_semaphore()
    for d in range(1, n_orb):
        pl.semaphore_signal(barrier, inc=1, device_id=(aux, lax.rem(orb + d, n_orb)), device_id_type=MESH)
    for d in range(1, n_aux):
        pl.semaphore_signal(barrier, inc=1, device_id=(lax.rem(aux + d, n_aux), orb), device_id_type=MESH)
    pl.semaphore_wait(barrier, n_orb - 1 + n_aux - 1)

    def load(t, base, buf, sem):
        g, u = t // per_group, lax.rem(t, per_group)
        start = pl.multiple_of(base * half + u * CHUNK_ROWS, 16)
        slot = lax.rem(t, SLOTS)
        return pltpu.make_async_copy(
            x_ref.at[pl.ds(g * 2, 2), pl.ds(start, CHUNK_ROWS), :], buf.at[slot], sem.at[slot]
        )

    def load_own(t):
        return load(t, core, xo, xo_sem)

    def load_other(t):
        return load(t, 1 - core, xp, xp_sem)

    def transform(t, buf):
        g = t // per_group
        slot = lax.rem(t, SLOTS)
        parts = []
        for k in range(2):
            parts.append(
                jnp.dot(buf[slot, k], coef_ref[g * 2 + k], preferred_element_type=jnp.float32)
            )
        return jnp.concatenate(parts, axis=1)

    def to_peer(t):
        return pltpu.make_async_remote_copy(
            psend.at[t], pin.at[t], ps_sem.at[t], pr_sem.at[t], device_id=(aux, peer), device_id_type=MESH
        )

    def to_next(t):
        return pltpu.make_async_remote_copy(
            zin.at[t], zin.at[t], zs_sem.at[t], zr_sem.at[t], device_id=(aux, following), device_id_type=MESH
        )

    def to_row_owner(par, idx, r, col):
        owner = r // row_groups
        d = lax.rem(aux - owner + n_aux, n_aux)
        d = jnp.maximum(d, 1)
        rl = lax.rem(r, row_groups)
        return pltpu.make_async_remote_copy(
            gsend.at[par, idx], grecv.at[d - 1, rl, col], gs_sem.at[par, idx], gr_sem.at[d - 1, rl, col],
            device_id=(owner, orb), device_id_type=MESH,
        )

    def to_owner(rl, col):
        return pltpu.make_async_remote_copy(
            gz.at[rl, col], gfin.at[core, rl], fs_sem.at[rl, col], fr_sem.at[core, rl],
            device_id=(aux, col), device_id_type=MESH,
        )

    def each_block(g, fn):
        def body(r, carry):
            fn(r, r, g)

            @pl.when(r < g)
            def _():
                fn(groups + r, g, r)

            return carry

        lax.fori_loop(0, g + 1, body, 0)

    def drain(g):
        par = lax.rem(g, 2)

        def one(idx, r, col):
            @pl.when(r // row_groups != aux)
            def _():
                to_row_owner(par, idx, r, col).wait_send()

        each_block(g, one)

    def gram(g):
        par = lax.rem(g, 2)

        @pl.when(g >= 2)
        def _():
            drain(g - 2)

        first = g * per_group
        bt[g] = zin[pl.ds(first, per_group)].reshape(half, GROUP).T

        def send(idx, r, col):
            @pl.when(r // row_groups != aux)
            def _():
                to_row_owner(par, idx, r, col).start()

        def body(r, carry):
            block = jnp.dot(
                bt[r], zin[pl.ds(first, per_group)].reshape(half, GROUP), preferred_element_type=jnp.float32
            )
            gsend[par, r] = block.astype(jnp.bfloat16)
            send(r, r, g)

            @pl.when(r < g)
            def _():
                gsend[par, groups + r] = block.T.astype(jnp.bfloat16)
                send(groups + r, g, r)

            return carry

        lax.fori_loop(0, g + 1, body, 0)

    def combine(g):
        par = lax.rem(g, 2)

        def one(idx, r, col):
            @pl.when(r // row_groups == aux)
            def _():
                rl = lax.rem(r, row_groups)
                acc = gsend[par, idx].astype(jnp.float32)
                for d in range(1, n_aux):
                    pltpu.make_async_remote_copy(
                        gsend.at[par, idx], grecv.at[d - 1, rl, col], gs_sem.at[par, idx],
                        gr_sem.at[d - 1, rl, col], device_id=(aux, peer), device_id_type=MESH,
                    ).wait_recv()
                    acc += grecv[d - 1, rl, col].astype(jnp.float32)
                value = acc.astype(jnp.bfloat16)

                @pl.when(col == orb)
                def _():
                    gfin[core, rl] = value

                @pl.when(col != orb)
                def _():
                    gz[rl, col] = value
                    to_owner(rl, col).start()

        each_block(g, one)

    for t in range(SLOTS):
        load_other(t).start()
        load_own(t).start()

    def step(t, carry):
        @pl.when(t < chunks)
        def _():
            load_other(t).wait()
            psend[t] = transform(t, xp).astype(jnp.bfloat16)
            to_peer(t).start()

            @pl.when(t + SLOTS < chunks)
            def _():
                load_other(t + SLOTS).start()

        @pl.when(t >= LEAD)
        def _():
            now = t - LEAD
            load_own(now).wait()
            own = transform(now, xo)

            @pl.when(now + SLOTS < chunks)
            def _():
                load_own(now + SLOTS).start()

            to_peer(now).wait_recv()
            own += pin[now].astype(jnp.float32)

            @pl.when(stage == 0)
            def _():
                zin[now] = own.astype(jnp.bfloat16)

            @pl.when(stage > 0)
            def _():
                to_next(now).wait_recv()
                zin[now] = (own + zin[now].astype(jnp.float32)).astype(jnp.bfloat16)

            @pl.when(jnp.logical_not(last))
            def _():
                @pl.when(now >= IN_FLIGHT)
                def _():
                    to_next(now - IN_FLIGHT).wait_send()

                to_next(now).start()

            @pl.when(jnp.logical_and(last, lax.rem(now, per_group) == per_group - 1))
            def _():
                g = now // per_group
                gram(g)

                @pl.when(g >= 1)
                def _():
                    combine(g - 1)

        return carry

    lax.fori_loop(0, chunks + LEAD, step, 0)

    @pl.when(last)
    def _():
        combine(groups - 1)

    for end in range(2):
        finisher = 2 * (chips - 1) if end == 0 else 1
        for rl in range(row_groups):
            @pl.when(orb != finisher)
            def _():
                pltpu.make_async_remote_copy(
                    gz.at[rl, 0], gfin.at[end, rl], fs_sem.at[rl, 0], fr_sem.at[end, rl],
                    device_id=(aux, peer), device_id_type=MESH,
                ).wait_recv()

    for rl in range(row_groups):
        total_ref[rl] = gfin[0, rl].astype(jnp.float32) + gfin[1, rl].astype(jnp.float32)

    def sent(t, carry):
        to_peer(t).wait_send()
        return carry

    lax.fori_loop(0, chunks, sent, 0)

    @pl.when(jnp.logical_not(last))
    def _():
        for k in range(IN_FLIGHT):
            to_next(chunks - IN_FLIGHT + k).wait_send()

    @pl.when(last)
    def _():
        if groups >= 2:
            drain(groups - 2)
        drain(groups - 1)

        def left(col, carry):
            @pl.when(col != orb)
            def _():
                for rl in range(row_groups):
                    to_owner(rl, col).wait_send()

            return carry

        lax.fori_loop(0, groups, left, 0)


def pick(dom_ref, coef_ref, chosen_ref):
    for i in range(chosen_ref.shape[0]):
        first = pl.multiple_of(dom_ref[i] * BS, BS)
        chosen_ref[i] = coef_ref[:, pl.ds(first, BS)]


def pair_totals(integrals, coeffs, domains):
    n_aux, n_orb = lax.axis_size("aux"), lax.axis_size("orb")
    occupied, aux_rows, ao_local = integrals.shape
    groups = occupied // 2
    half = aux_rows // 2
    per_group = half // CHUNK_ROWS
    chunks = groups * per_group
    row_groups = occupied // n_aux // 2
    assert groups == n_orb and half % CHUNK_ROWS == 0
    dims = (n_aux, n_orb, groups, per_group, row_groups)
    bf16 = jnp.bfloat16
    chosen = pl.pallas_call(
        pick,
        out_shape=jax.ShapeDtypeStruct((occupied, ao_local, BS), bf16),
        in_specs=[pl.BlockSpec(memory_space=pltpu.SMEM), pl.BlockSpec(memory_space=pltpu.VMEM)],
        out_specs=pl.BlockSpec(memory_space=pltpu.VMEM),
    )(domains, coeffs)
    vmem = pltpu.VMEM
    dma = pltpu.SemaphoreType.DMA
    return pl.pallas_call(
        functools.partial(exchange, dims),
        out_shape=jax.ShapeDtypeStruct((row_groups, GROUP, GROUP), jnp.float32),
        in_specs=[
            pl.BlockSpec(memory_space=pltpu.VMEM),
            pl.BlockSpec(memory_space=pl.ANY),
        ],
        out_specs=pl.BlockSpec(memory_space=pltpu.VMEM),
        scratch_shapes=[
            vmem((SLOTS, 2, CHUNK_ROWS, ao_local), bf16),
            vmem((SLOTS, 2, CHUNK_ROWS, ao_local), bf16),
            vmem((chunks, CHUNK_ROWS, GROUP), bf16),
            vmem((chunks, CHUNK_ROWS, GROUP), bf16),
            vmem((chunks, CHUNK_ROWS, GROUP), bf16),
            vmem((groups, GROUP, half), bf16),
            vmem((2, 2 * groups, GROUP, GROUP), bf16),
            vmem((n_aux - 1, row_groups, groups, GROUP, GROUP), bf16),
            vmem((row_groups, groups, GROUP, GROUP), bf16),
            vmem((2, row_groups, GROUP, GROUP), bf16),
            dma((SLOTS,)),
            dma((SLOTS,)),
            dma((chunks,)),
            dma((chunks,)),
            dma((chunks,)),
            dma((chunks,)),
            dma((2, 2 * groups)),
            dma((n_aux - 1, row_groups, groups)),
            dma((row_groups, groups)),
            dma((2, row_groups)),
        ],
        compiler_params=pltpu.CompilerParams(
            collective_id=0, has_side_effects=True, vmem_limit_bytes=62 * 1024 * 1024
        ),
        cost_estimate=pl.CostEstimate(
            flops=2 * occupied * aux_rows * ao_local * BS, bytes_accessed=2 * integrals.size, transcendentals=0
        ),
    )(chosen, integrals)


def shards(integrals, coeffs, domains, eps_occ, eps_vir, pair_mask):
    occupied = integrals.shape[0]
    vir_blocks = coeffs.shape[1] // BS
    own_count = occupied // lax.axis_size("orb")
    row_count = occupied // lax.axis_size("aux")
    aux_index = lax.axis_index("aux")
    orb_index = lax.axis_index("orb")
    totals = pair_totals(integrals, coeffs, domains).reshape(row_count, BS, own_count, BS)
    pair_ints = totals * (1.0 / jnp.sqrt(jnp.float32(NAUX)))
    selector = domains[:, None] == jnp.arange(vir_blocks, dtype=jnp.int32)[None, :]
    vir_energy = jnp.dot(
        selector.astype(jnp.float32),
        eps_vir.reshape(vir_blocks, BS),
        precision=lax.Precision.HIGHEST,
    )
    vir_rows = lax.dynamic_slice_in_dim(vir_energy, aux_index * row_count, row_count, 0)
    vir_cols = lax.dynamic_slice_in_dim(vir_energy, orb_index * own_count, own_count, 0)
    occ_rows = lax.dynamic_slice_in_dim(eps_occ, aux_index * row_count, row_count, 0)
    occ_cols = lax.dynamic_slice_in_dim(eps_occ, orb_index * own_count, own_count, 0)
    denominator = (
        vir_rows[:, :, None, None]
        + vir_cols[None, None, :, :]
        - occ_rows[:, None, None, None]
        - occ_cols[None, None, :, None]
    )
    screen = pair_mask.astype(jnp.float32)
    amplitudes = screen[:, None, :, None] * pair_ints / denominator
    energies = -jnp.sum(pair_ints * amplitudes, axis=(1, 3)) / float(BS * BS)
    return (amplitudes.astype(jnp.bfloat16), energies)


def solution(mesh):
    return jax.shard_map(
        shards,
        mesh=mesh,
        in_specs=(P(None, "aux", "orb"), P("orb", None), P(), P(), P(), P("aux", "orb")),
        out_specs=(P("aux", None, "orb", None), P("aux", "orb")),
        check_vma=False,
    )
```

time: 382 us -> 221 us (0.58)
  waiting for transfers between devices: 326 us -> 0 us
  Pallas kernels: 0 us -> 214 us
  matrix products: 29.7 us -> 0.19 us
  between operations: 13.8 us -> 0.72 us
  local copies, waits for them, and re-layouts: 8.13 us -> 2.24 us
    pallas_call x0 -> x2, Pallas kernels: none -> 214 us  [the longest x1 211 us: pair_totals(): pl.pallas_call(functools.partial(exchange, dims), out_shape=jax.ShapeDtyp...]
    reduce_scatter x2 -> x0, waiting for transfers between devices: 184 us -> none  [the longest x1 158 us: shards(): lax.psum_scatter(jnp.einsum('ipm,imb->ipb', integrals, chosen, preferred_...]
    all_gather x1 -> x0, waiting for transfers between devices: 141 us -> none  [shards(): all_blocks = lax.all_gather(own_blocks, 'orb', axis=0, tiled=True)]
    dot_general x3 -> x0, matrix products: 29.5 us -> none  [the longest x1 19.3 us: shards(): jnp.einsum('ipm,imb->ipb', integrals, chosen, preferred_element_type=jnp....]
    reduce_scatter x1 -> x0, local copies, waits for them, and re-layouts: 3.97 us -> none  [shards(): lax.psum_scatter(jnp.einsum('ipm,imb->ipb', integrals, chosen, preferred_...]
  transfers between devices with their start and end apart: 3 -> 0, of which waited for: 3 -> 0; matrix products, arithmetic and copies ran while one was open for 0% -> 0% of each run, Pallas kernels for 0% -> 0%
where the time goes in v1:
time: 221 us; the launch traced here: 218 us
  Pallas kernels  214 us (97%)
  local copies, waits for them, and re-layouts  2.24 us (1%)
    pallas_call x1, Pallas kernels, pair_totals(): pl.pallas_call(functools.partial(exchange, dims), out_shape=jax.ShapeDtyp...  211 us

profile of v1, /device:TPU:23, one launch (start us, length us, event | category | flops | bytes accessed | tf_op | source)
XLA Modules:
  0.0 218.5 jit_solution(9364499649444806716)
XLA Ops:
  0.6 0.0 copy-start
  0.6 0.0 copy-start.2
  0.7 0.0 copy-start.3
  0.7 0.0 copy-start.1
  0.7 2.5 %shard_map.77.coef_ref = bf16[16,256,128]{2,1,0:T(8,128)(2,1)} custom-call(s32[16]{0:T(128)} %dom_ref.1, bf16[256,2048]{1,0:T(8,128)(2,1)} %coef_ref.1), custom_call_target="tpu_custom_call" | custom-call | tf_op jit(solution)/shard_map/pallas_call | solution.py:296
  3.2 211.2 %shard_map.78 = f32[2,256,256]{2,1,0:T(8,128)} custom-call(bf16[16,256,128]{2,1,0:T(8,128)(2,1)} %shard_map.77.coef_ref, bf16[16,3840,256]{2,1,0:T(8,128)(2,1)} %x_ref.1), custom_call_target="tpu_custom_call" | custom-call | flops 4026531840 | bytes 31457280 | tf_op jit(solution)/shard_map/pallas_call | solution.py:304
  214.4 1.3 reshape.16
  215.7 0.0 copy-done.3
  215.7 0.1 dynamic_slice.15
  215.8 0.1 dynamic_slice.14
  215.8 0.0 copy-done
  215.8 0.0 copy-done.2
  215.8 0.2 fusion
  216.1 0.0 copy-done.1
  216.1 0.1 copy.9
  216.2 1.6 multiply_reduce_fusion
  217.8 0.7 copy.10
  (4 shorter events, 0.0 us)
Async XLA Ops:
  0.6 215.2 %copy-start = (f32[2048]{0:T(1024)S(1)}, f32[2048]{0:T(1024)}, u32[]{:S(2)}) copy-start(f32[2048]{0:T(1024)} %param.10) | copy-start | bytes 24580
  0.6 215.2 %copy-start.2 = (s32[16]{0:T(128)S(1)}, s32[16]{0:T(128)}, u32[]{:S(2)}) copy-start(s32[16]{0:T(128)} %dom_ref.1) | copy-start | bytes 196
  0.7 215.0 %copy-start.3 = (f32[16]{0:T(128)S(1)}, f32[16]{0:T(128)}, u32[]{:S(2)}) copy-start(f32[16]{0:T(128)} %param.9) | copy-start | bytes 196
  0.7 215.4 %copy-start.1 = (s32[4,2]{0,1:T(2,128)S(1)}, s32[4,2]{0,1:T(2,128)}, u32[]{:S(2)}) copy-start(s32[4,2]{0,1:T(2,128)} %param.11) | copy-start | bytes 100

commit v2 on v1

--- a/solution.py
+++ b/solution.py
@@ -11,8 +11,9 @@
 BS = 128
 GROUP = 2 * BS
 CHUNK_ROWS = 240
-LEAD = 4
+LEAD = 6
 SLOTS = 4
+OTHER_SLOTS = 8
 IN_FLIGHT = 4
 MESH = pl.DeviceIdType.MESH
 
@@ -43,23 +44,23 @@
         pl.semaphore_signal(barrier, inc=1, device_id=(lax.rem(aux + d, n_aux), orb), device_id_type=MESH)
     pl.semaphore_wait(barrier, n_orb - 1 + n_aux - 1)
 
-    def load(t, base, buf, sem):
+    def load(t, base, buf, sem, slots):
         g, u = t // per_group, lax.rem(t, per_group)
         start = pl.multiple_of(base * half + u * CHUNK_ROWS, 16)
-        slot = lax.rem(t, SLOTS)
+        slot = lax.rem(t, slots)
         return pltpu.make_async_copy(
             x_ref.at[pl.ds(g * 2, 2), pl.ds(start, CHUNK_ROWS), :], buf.at[slot], sem.at[slot]
         )
 
     def load_own(t):
-        return load(t, core, xo, xo_sem)
+        return load(t, core, xo, xo_sem, SLOTS)
 
     def load_other(t):
-        return load(t, 1 - core, xp, xp_sem)
-
-    def transform(t, buf):
+        return load(t, 1 - core, xp, xp_sem, OTHER_SLOTS)
+
+    def transform(t, buf, slots):
         g = t // per_group
-        slot = lax.rem(t, SLOTS)
+        slot = lax.rem(t, slots)
         parts = []
         for k in range(2):
             parts.append(
@@ -123,28 +124,27 @@
             drain(g - 2)
 
         first = g * per_group
-        bt[g] = zin[pl.ds(first, per_group)].reshape(half, GROUP).T
 
         def send(idx, r, col):
             @pl.when(r // row_groups != aux)
             def _():
                 to_row_owner(par, idx, r, col).start()
 
+        def column():
+            return zin[pl.ds(first, per_group)].reshape(half, GROUP)
+
         def body(r, carry):
-            block = jnp.dot(
-                bt[r], zin[pl.ds(first, per_group)].reshape(half, GROUP), preferred_element_type=jnp.float32
-            )
+            block = jnp.dot(bt[r], column(), preferred_element_type=jnp.float32)
             gsend[par, r] = block.astype(jnp.bfloat16)
             send(r, r, g)
-
-            @pl.when(r < g)
-            def _():
-                gsend[par, groups + r] = block.T.astype(jnp.bfloat16)
-                send(groups + r, g, r)
-
+            gsend[par, groups + r] = block.T.astype(jnp.bfloat16)
+            send(groups + r, g, r)
             return carry
 
-        lax.fori_loop(0, g + 1, body, 0)
+        lax.fori_loop(0, g, body, 0)
+        bt[g] = column().T
+        gsend[par, g] = jnp.dot(bt[g], column(), preferred_element_type=jnp.float32).astype(jnp.bfloat16)
+        send(g, g, g)
 
     def combine(g):
         par = lax.rem(g, 2)
@@ -173,63 +173,73 @@
 
         each_block(g, one)
 
+    for t in range(OTHER_SLOTS):
+        load_other(t).start()
     for t in range(SLOTS):
-        load_other(t).start()
         load_own(t).start()
 
-    def step(t, carry):
-        @pl.when(t < chunks)
-        def _():
-            load_other(t).wait()
-            psend[t] = transform(t, xp).astype(jnp.bfloat16)
-            to_peer(t).start()
-
-            @pl.when(t + SLOTS < chunks)
-            def _():
-                load_other(t + SLOTS).start()
-
-        @pl.when(t >= LEAD)
-        def _():
-            now = t - LEAD
-            load_own(now).wait()
-            own = transform(now, xo)
-
-            @pl.when(now + SLOTS < chunks)
-            def _():
-                load_own(now + SLOTS).start()
-
-            to_peer(now).wait_recv()
-            own += pin[now].astype(jnp.float32)
-
-            @pl.when(stage == 0)
-            def _():
-                zin[now] = own.astype(jnp.bfloat16)
-
-            @pl.when(stage > 0)
-            def _():
-                to_next(now).wait_recv()
-                zin[now] = (own + zin[now].astype(jnp.float32)).astype(jnp.bfloat16)
-
-            @pl.when(jnp.logical_not(last))
-            def _():
-                @pl.when(now >= IN_FLIGHT)
-                def _():
-                    to_next(now - IN_FLIGHT).wait_send()
-
-                to_next(now).start()
-
-            @pl.when(jnp.logical_and(last, lax.rem(now, per_group) == per_group - 1))
-            def _():
-                g = now // per_group
-                gram(g)
-
-                @pl.when(g >= 1)
-                def _():
-                    combine(g - 1)
-
+    def help_peer(t):
+        load_other(t).wait()
+        psend[t] = transform(t, xp, OTHER_SLOTS).astype(jnp.bfloat16)
+        to_peer(t).start()
+
+        @pl.when(t + OTHER_SLOTS < chunks)
+        def _():
+            load_other(t + OTHER_SLOTS).start()
+
+    def ahead(t, carry):
+        help_peer(t)
         return carry
 
-    lax.fori_loop(0, chunks + LEAD, step, 0)
+    lax.fori_loop(0, LEAD, ahead, 0)
+
+    def step(now, carry):
+        for k in range(2):
+            t = LEAD + 2 * now + k
+
+            @pl.when(t < chunks)
+            def _():
+                help_peer(t)
+
+        load_own(now).wait()
+        own = transform(now, xo, SLOTS)
+
+        @pl.when(now + SLOTS < chunks)
+        def _():
+            load_own(now + SLOTS).start()
+
+        to_peer(now).wait_recv()
+        own += pin[now].astype(jnp.float32)
+
+        @pl.when(stage == 0)
+        def _():
+            zin[now] = own.astype(jnp.bfloat16)
+
+        @pl.when(stage > 0)
+        def _():
+            to_next(now).wait_recv()
+            zin[now] = (own + zin[now].astype(jnp.float32)).astype(jnp.bfloat16)
+
+        @pl.when(jnp.logical_not(last))
+        def _():
+            @pl.when(now >= IN_FLIGHT)
+            def _():
+                to_next(now - IN_FLIGHT).wait_send()
+
+            to_next(now).start()
+
+        @pl.when(jnp.logical_and(last, lax.rem(now, per_group) == per_group - 1))
+        def _():
+            g = now // per_group
+            gram(g)
+
+            @pl.when(g >= 1)
+            def _():
+                combine(g - 1)
+
+        return carry
+
+    lax.fori_loop(0, chunks, step, 0)
 
     @pl.when(last)
     def _():
@@ -311,7 +321,7 @@
         out_specs=pl.BlockSpec(memory_space=pltpu.VMEM),
         scratch_shapes=[
             vmem((SLOTS, 2, CHUNK_ROWS, ao_local), bf16),
-            vmem((SLOTS, 2, CHUNK_ROWS, ao_local), bf16),
+            vmem((OTHER_SLOTS, 2, CHUNK_ROWS, ao_local), bf16),
             vmem((chunks, CHUNK_ROWS, GROUP), bf16),
             vmem((chunks, CHUNK_ROWS, GROUP), bf16),
             vmem((chunks, CHUNK_ROWS, GROUP), bf16),
@@ -321,7 +331,7 @@
             vmem((row_groups, groups, GROUP, GROUP), bf16),
             vmem((2, row_groups, GROUP, GROUP), bf16),
             dma((SLOTS,)),
-            dma((SLOTS,)),
+            dma((OTHER_SLOTS,)),
             dma((chunks,)),
             dma((chunks,)),
             dma((chunks,)),

time: 221 us -> 168 us (0.76)
  the two profiles are of different devices: /device:TPU:23 before, /device:TPU:31 now
where the time goes in v2:
time: 168 us
  Pallas kernels  163 us (97%)
  local copies, waits for them, and re-layouts  2.24 us (1%)
    pallas_call x1, Pallas kernels, pair_totals(): pl.pallas_call(functools.partial(exchange, dims), out_shape=jax.ShapeDtyp...  160 us

profile of v2, /device:TPU:31, one launch (start us, length us, event | category | flops | bytes accessed | tf_op | source)
XLA Modules:
  0.0 167.6 jit_solution(2235919991477474487)
XLA Ops:
  0.6 0.0 copy-start
  0.6 0.0 copy-start.2
  0.7 0.0 copy-start.3
  0.7 0.0 copy-start.1
  0.7 2.5 %shard_map.77.coef_ref = bf16[16,256,128]{2,1,0:T(8,128)(2,1)} custom-call(s32[16]{0:T(128)} %dom_ref.1, bf16[256,2048]{1,0:T(8,128)(2,1)} %coef_ref.1), custom_call_target="tpu_custom_call" | custom-call | tf_op jit(solution)/shard_map/pallas_call | solution.py:306
  3.2 160.4 %shard_map.78 = f32[2,256,256]{2,1,0:T(8,128)} custom-call(bf16[16,256,128]{2,1,0:T(8,128)(2,1)} %shard_map.77.coef_ref, bf16[16,3840,256]{2,1,0:T(8,128)(2,1)} %x_ref.1), custom_call_target="tpu_custom_call" | custom-call | flops 4026531840 | bytes 31457280 | tf_op jit(solution)/shard_map/pallas_call | solution.py:314
  163.5 1.3 reshape.16
  164.8 0.0 copy-done.3
  164.9 0.1 dynamic_slice.15
  164.9 0.1 dynamic_slice.14
  165.0 0.0 copy-done
  165.0 0.0 copy-done.2
  165.0 0.2 fusion
  165.2 0.0 copy-done.1
  165.3 0.1 copy.9
  165.3 1.6 multiply_reduce_fusion
  167.0 0.7 copy.10
  (4 shorter events, 0.0 us)
Async XLA Ops:
  0.6 164.4 %copy-start = (f32[2048]{0:T(1024)S(1)}, f32[2048]{0:T(1024)}, u32[]{:S(2)}) copy-start(f32[2048]{0:T(1024)} %param.10) | copy-start | bytes 24580
  0.6 164.4 %copy-start.2 = (s32[16]{0:T(128)S(1)}, s32[16]{0:T(128)}, u32[]{:S(2)}) copy-start(s32[16]{0:T(128)} %dom_ref.1) | copy-start | bytes 196
  0.7 164.2 %copy-start.3 = (f32[16]{0:T(128)S(1)}, f32[16]{0:T(128)}, u32[]{:S(2)}) copy-start(f32[16]{0:T(128)} %param.9) | copy-start | bytes 196
  0.7 164.6 %copy-start.1 = (s32[4,2]{0,1:T(2,128)S(1)}, s32[4,2]{0,1:T(2,128)}, u32[]{:S(2)}) copy-start(s32[4,2]{0,1:T(2,128)} %param.11) | copy-start | bytes 100

commit v3 on v2

--- a/solution.py
+++ b/solution.py
@@ -21,8 +21,8 @@
 def exchange(
     dims,
     coef_ref, x_ref, total_ref,
-    xo, xp, zin, pin, psend, bt, gsend, grecv, gz, gfin,
-    xo_sem, xp_sem, ps_sem, pr_sem, zs_sem, zr_sem, gs_sem, gr_sem, fs_sem, fr_sem,
+    xo, xp, zin, pin, psend, bt, gsend, grecv, gz, gzt, gfin, gin, ffin,
+    xo_sem, xp_sem, ps_sem, pr_sem, zs_sem, zr_sem, gs_sem, gr_sem, fs_sem, fr_sem, ts_sem, tr_sem, ws_sem, wr_sem,
 ):
     n_aux, n_orb, groups, per_group, row_groups = dims
     chips = n_orb // 2
@@ -78,43 +78,54 @@
             zin.at[t], zin.at[t], zs_sem.at[t], zr_sem.at[t], device_id=(aux, following), device_id_type=MESH
         )
 
-    def to_row_owner(par, idx, r, col):
-        owner = r // row_groups
-        d = lax.rem(aux - owner + n_aux, n_aux)
-        d = jnp.maximum(d, 1)
-        rl = lax.rem(r, row_groups)
-        return pltpu.make_async_remote_copy(
-            gsend.at[par, idx], grecv.at[d - 1, rl, col], gs_sem.at[par, idx], gr_sem.at[d - 1, rl, col],
+    def line_of(r):
+        return r // row_groups
+
+    def native(a, b):
+        lo, hi = jnp.minimum(a, b), jnp.maximum(a, b)
+        takes_hi = jnp.logical_and(hi != groups - 1, lax.rem(lo, 2) == 1)
+        return jnp.where(takes_hi, hi, lo)
+
+    def to_reducer(par, r, g):
+        n = native(r, g)
+        m = r + g - n
+        owner = line_of(n)
+        d = jnp.maximum(lax.rem(aux - owner + n_aux, n_aux), 1)
+        rl = lax.rem(n, row_groups)
+        return pltpu.make_async_remote_copy(
+            gsend.at[par, r], grecv.at[d - 1, rl, m], gs_sem.at[par, r], gr_sem.at[d - 1, rl, m],
             device_id=(owner, orb), device_id_type=MESH,
         )
 
-    def to_owner(rl, col):
-        return pltpu.make_async_remote_copy(
-            gz.at[rl, col], gfin.at[core, rl], fs_sem.at[rl, col], fr_sem.at[core, rl],
-            device_id=(aux, col), device_id_type=MESH,
-        )
-
-    def each_block(g, fn):
-        def body(r, carry):
-            fn(r, r, g)
-
-            @pl.when(r < g)
-            def _():
-                fn(groups + r, g, r)
-
-            return carry
-
-        lax.fori_loop(0, g + 1, body, 0)
+    def to_owner(rl, m):
+        return pltpu.make_async_remote_copy(
+            gz.at[rl, m], gfin.at[core, rl], fs_sem.at[rl, m], fr_sem.at[core, rl],
+            device_id=(aux, m), device_id_type=MESH,
+        )
+
+    def to_forwarder(rl, m, n):
+        return pltpu.make_async_remote_copy(
+            gzt.at[rl, m], gin.at[core, m], ts_sem.at[rl, m], tr_sem.at[core, m],
+            device_id=(aux, n), device_id_type=MESH,
+        )
+
+    def forward(m):
+        return pltpu.make_async_remote_copy(
+            gin.at[0, m], ffin.at[lax.rem(m, row_groups)], ws_sem.at[m], wr_sem.at[lax.rem(m, row_groups)],
+            device_id=(line_of(m), orb), device_id_type=MESH,
+        )
 
     def drain(g):
         par = lax.rem(g, 2)
 
-        def one(idx, r, col):
-            @pl.when(r // row_groups != aux)
-            def _():
-                to_row_owner(par, idx, r, col).wait_send()
-
-        each_block(g, one)
+        def body(r, carry):
+            @pl.when(line_of(native(r, g)) != aux)
+            def _():
+                to_reducer(par, r, g).wait_send()
+
+            return carry
+
+        lax.fori_loop(0, g + 1, body, 0)
 
     def gram(g):
         par = lax.rem(g, 2)
@@ -125,53 +136,74 @@
 
         first = g * per_group
 
-        def send(idx, r, col):
-            @pl.when(r // row_groups != aux)
-            def _():
-                to_row_owner(par, idx, r, col).start()
-
         def column():
             return zin[pl.ds(first, per_group)].reshape(half, GROUP)
 
+        def block(r):
+            gsend[par, r] = jnp.dot(bt[r], column(), preferred_element_type=jnp.float32).astype(jnp.bfloat16)
+
+            @pl.when(line_of(native(r, g)) != aux)
+            def _():
+                to_reducer(par, r, g).start()
+
         def body(r, carry):
-            block = jnp.dot(bt[r], column(), preferred_element_type=jnp.float32)
-            gsend[par, r] = block.astype(jnp.bfloat16)
-            send(r, r, g)
-            gsend[par, groups + r] = block.T.astype(jnp.bfloat16)
-            send(groups + r, g, r)
+            block(r)
             return carry
 
         lax.fori_loop(0, g, body, 0)
         bt[g] = column().T
-        gsend[par, g] = jnp.dot(bt[g], column(), preferred_element_type=jnp.float32).astype(jnp.bfloat16)
-        send(g, g, g)
+        block(g)
 
     def combine(g):
         par = lax.rem(g, 2)
 
-        def one(idx, r, col):
-            @pl.when(r // row_groups == aux)
-            def _():
-                rl = lax.rem(r, row_groups)
-                acc = gsend[par, idx].astype(jnp.float32)
+        def body(r, carry):
+            n = native(r, g)
+            m = r + g - n
+            rl = lax.rem(n, row_groups)
+
+            @pl.when(line_of(n) == aux)
+            def _():
+                acc = gsend[par, r].astype(jnp.float32)
                 for d in range(1, n_aux):
                     pltpu.make_async_remote_copy(
-                        gsend.at[par, idx], grecv.at[d - 1, rl, col], gs_sem.at[par, idx],
-                        gr_sem.at[d - 1, rl, col], device_id=(aux, peer), device_id_type=MESH,
+                        gsend.at[par, r], grecv.at[d - 1, rl, m], gs_sem.at[par, r], gr_sem.at[d - 1, rl, m],
+                        device_id=(aux, peer), device_id_type=MESH,
                     ).wait_recv()
-                    acc += grecv[d - 1, rl, col].astype(jnp.float32)
-                value = acc.astype(jnp.bfloat16)
-
-                @pl.when(col == orb)
+                    acc += grecv[d - 1, rl, m].astype(jnp.float32)
+
+                def deliver(straight, turned):
+                    @pl.when(m == orb)
+                    def _():
+                        gfin[core, rl] = straight().astype(jnp.bfloat16)
+
+                    @pl.when(m != orb)
+                    def _():
+                        gz[rl, m] = straight().astype(jnp.bfloat16)
+                        to_owner(rl, m).start()
+
+                    @pl.when(m != n)
+                    def _():
+                        @pl.when(n == orb)
+                        def _():
+                            gin[core, m] = turned().astype(jnp.bfloat16)
+
+                        @pl.when(n != orb)
+                        def _():
+                            gzt[rl, m] = turned().astype(jnp.bfloat16)
+                            to_forwarder(rl, m, n).start()
+
+                @pl.when(n == r)
                 def _():
-                    gfin[core, rl] = value
-
-                @pl.when(col != orb)
+                    deliver(lambda: acc, lambda: acc.T)
+
+                @pl.when(n != r)
                 def _():
-                    gz[rl, col] = value
-                    to_owner(rl, col).start()
-
-        each_block(g, one)
+                    deliver(lambda: acc.T, lambda: acc)
+
+            return carry
+
+        lax.fori_loop(0, g + 1, body, 0)
 
     for t in range(OTHER_SLOTS):
         load_other(t).start()
@@ -228,14 +260,15 @@
 
             to_next(now).start()
 
+        g = now // per_group
+
+        @pl.when(jnp.logical_and(jnp.logical_and(last, g >= 1), lax.rem(now, per_group) == per_group // 2))
+        def _():
+            combine(g - 1)
+
         @pl.when(jnp.logical_and(last, lax.rem(now, per_group) == per_group - 1))
         def _():
-            g = now // per_group
             gram(g)
-
-            @pl.when(g >= 1)
-            def _():
-                combine(g - 1)
 
         return carry
 
@@ -245,18 +278,58 @@
     def _():
         combine(groups - 1)
 
-    for end in range(2):
-        finisher = 2 * (chips - 1) if end == 0 else 1
-        for rl in range(row_groups):
-            @pl.when(orb != finisher)
-            def _():
-                pltpu.make_async_remote_copy(
-                    gz.at[rl, 0], gfin.at[end, rl], fs_sem.at[rl, 0], fr_sem.at[end, rl],
-                    device_id=(aux, peer), device_id_type=MESH,
-                ).wait_recv()
+    finishers = (2 * (chips - 1), 1)
+
+    def pass_on(m, carry):
+        @pl.when(jnp.logical_and(m != orb, native(orb, m) == orb))
+        def _():
+            for end in range(2):
+                @pl.when(orb != finishers[end])
+                def _():
+                    pltpu.make_async_remote_copy(
+                        gzt.at[0, 0], gin.at[end, m], ts_sem.at[0, 0], tr_sem.at[end, m],
+                        device_id=(aux, peer), device_id_type=MESH,
+                    ).wait_recv()
+
+            both = gin[0, m].astype(jnp.float32) + gin[1, m].astype(jnp.float32)
+
+            @pl.when(line_of(m) == aux)
+            def _():
+                total_ref[lax.rem(m, row_groups)] = both
+
+            @pl.when(line_of(m) != aux)
+            def _():
+                gin[0, m] = both.astype(jnp.bfloat16)
+                forward(m).start()
+
+        return carry
+
+    @pl.when(line_of(orb) == aux)
+    def _():
+        lax.fori_loop(0, groups, pass_on, 0)
 
     for rl in range(row_groups):
-        total_ref[rl] = gfin[0, rl].astype(jnp.float32) + gfin[1, rl].astype(jnp.float32)
+        r = aux * row_groups + rl
+
+        @pl.when(native(r, orb) == r)
+        def _():
+            for end in range(2):
+                @pl.when(orb != finishers[end])
+                def _():
+                    pltpu.make_async_remote_copy(
+                        gz.at[rl, 0], gfin.at[end, rl], fs_sem.at[rl, 0], fr_sem.at[end, rl],
+                        device_id=(aux, peer), device_id_type=MESH,
+                    ).wait_recv()
+
+            total_ref[rl] = gfin[0, rl].astype(jnp.float32) + gfin[1, rl].astype(jnp.float32)
+
+        @pl.when(jnp.logical_and(native(r, orb) != r, line_of(orb) != aux))
+        def _():
+            pltpu.make_async_remote_copy(
+                gin.at[0, 0], ffin.at[rl], ws_sem.at[0], wr_sem.at[rl],
+                device_id=(aux, peer), device_id_type=MESH,
+            ).wait_recv()
+            total_ref[rl] = ffin[rl].astype(jnp.float32)
 
     def sent(t, carry):
         to_peer(t).wait_send()
@@ -275,15 +348,34 @@
             drain(groups - 2)
         drain(groups - 1)
 
-        def left(col, carry):
-            @pl.when(col != orb)
-            def _():
-                for rl in range(row_groups):
-                    to_owner(rl, col).wait_send()
+        def left(m, carry):
+            for rl in range(row_groups):
+                n = aux * row_groups + rl
+
+                @pl.when(native(n, m) == n)
+                def _():
+                    @pl.when(m != orb)
+                    def _():
+                        to_owner(rl, m).wait_send()
+
+                    @pl.when(jnp.logical_and(m != n, n != orb))
+                    def _():
+                        to_forwarder(rl, m, n).wait_send()
 
             return carry
 
         lax.fori_loop(0, groups, left, 0)
+
+    @pl.when(line_of(orb) == aux)
+    def _():
+        def passed(m, carry):
+            @pl.when(jnp.logical_and(native(orb, m) == orb, line_of(m) != aux))
+            def _():
+                forward(m).wait_send()
+
+            return carry
+
+        lax.fori_loop(0, groups, passed, 0)
 
 
 def pick(dom_ref, coef_ref, chosen_ref):
@@ -326,20 +418,27 @@
             vmem((chunks, CHUNK_ROWS, GROUP), bf16),
             vmem((chunks, CHUNK_ROWS, GROUP), bf16),
             vmem((groups, GROUP, half), bf16),
-            vmem((2, 2 * groups, GROUP, GROUP), bf16),
+            vmem((2, groups, GROUP, GROUP), bf16),
             vmem((n_aux - 1, row_groups, groups, GROUP, GROUP), bf16),
             vmem((row_groups, groups, GROUP, GROUP), bf16),
+            vmem((row_groups, groups, GROUP, GROUP), bf16),
             vmem((2, row_groups, GROUP, GROUP), bf16),
+            vmem((2, groups, GROUP, GROUP), bf16),
+            vmem((row_groups, GROUP, GROUP), bf16),
             dma((SLOTS,)),
             dma((OTHER_SLOTS,)),
             dma((chunks,)),
             dma((chunks,)),
             dma((chunks,)),
             dma((chunks,)),
-            dma((2, 2 * groups)),
+            dma((2, groups)),
             dma((n_aux - 1, row_groups, groups)),
             dma((row_groups, groups)),
             dma((2, row_groups)),
+            dma((row_groups, groups)),
+            dma((2, groups)),
+            dma((groups,)),
+            dma((row_groups,)),
         ],
         compiler_params=pltpu.CompilerParams(
             collective_id=0, has_side_effects=True, vmem_limit_bytes=62 * 1024 * 1024

time: 168 us -> 151 us (0.90)
  the two profiles are of different devices: /device:TPU:31 before, /device:TPU:23 now
where the time goes in v3:
time: 151 us
  Pallas kernels  146 us (97%)
  local copies, waits for them, and re-layouts  2.24 us (1%)
  other arithmetic  1.65 us (1%)
    pallas_call x1, Pallas kernels, pair_totals(): pl.pallas_call(functools.partial(exchange, dims), out_shape=jax.ShapeDtyp...  143 us

profile of v3, /device:TPU:23, one launch (start us, length us, event | category | flops | bytes accessed | tf_op | source)
XLA Modules:
  0.0 150.7 jit_solution(3271582735296132842)
XLA Ops:
  0.6 0.0 copy-start
  0.6 0.0 copy-start.2
  0.7 0.0 copy-start.3
  0.7 0.0 copy-start.1
  0.7 2.5 %shard_map.77.coef_ref = bf16[16,256,128]{2,1,0:T(8,128)(2,1)} custom-call(s32[16]{0:T(128)} %dom_ref.1, bf16[256,2048]{1,0:T(8,128)(2,1)} %coef_ref.1), custom_call_target="tpu_custom_call" | custom-call | tf_op jit(solution)/shard_map/pallas_call | solution.py:398
  3.2 143.4 %shard_map.78 = f32[2,256,256]{2,1,0:T(8,128)} custom-call(bf16[16,256,128]{2,1,0:T(8,128)(2,1)} %shard_map.77.coef_ref, bf16[16,3840,256]{2,1,0:T(8,128)(2,1)} %x_ref.1), custom_call_target="tpu_custom_call" | custom-call | flops 4026531840 | bytes 31457280 | tf_op jit(solution)/shard_map/pallas_call | solution.py:406
  146.6 1.3 reshape.16
  147.9 0.0 copy-done.3
  147.9 0.1 dynamic_slice.15
  148.0 0.1 dynamic_slice.14
  148.0 0.0 copy-done
  148.1 0.0 copy-done.2
  148.1 0.2 fusion
  148.3 0.0 copy-done.1
  148.3 0.1 copy.9
  148.4 1.6 %multiply_reduce_fusion = (f32[4,2]{1,0:T(4,128)S(1)}, bf16[4,128,2,128]{3,2,1,0:T(2,128)(2,1)}) fusion(f32[4,128,2,128]{3,2,1,0:T(2,128)S(1)} %reshape.16, f32[2]{0:T(128)S(1)} %dynamic_slice.15, f32[4]{0:T(128)S(1)} %dynamic_slice.14, f32[2,128]{1,0:T(2,128)S(1)} %constant_dynamic-slice_fusion, f32[4,128]{1,0:T(4,128)S(1)} %constant_dynamic-slice_fusion.1, ...), kind=kLoop, calls=%fused_computation | loop fusion | flops 1179640 | bytes 789592 | tf_op jit(solution)/shard_map/reduce_sum | solution.py:479
  150.0 0.7 copy.10
  (4 shorter events, 0.0 us)
Async XLA Ops:
  0.6 147.4 %copy-start = (f32[2048]{0:T(1024)S(1)}, f32[2048]{0:T(1024)}, u32[]{:S(2)}) copy-start(f32[2048]{0:T(1024)} %param.10) | copy-start | bytes 24580
  0.6 147.4 %copy-start.2 = (s32[16]{0:T(128)S(1)}, s32[16]{0:T(128)}, u32[]{:S(2)}) copy-start(s32[16]{0:T(128)} %dom_ref.1) | copy-start | bytes 196
  0.7 147.2 %copy-start.3 = (f32[16]{0:T(128)S(1)}, f32[16]{0:T(128)}, u32[]{:S(2)}) copy-start(f32[16]{0:T(128)} %param.9) | copy-start | bytes 196
  0.7 147.6 %copy-start.1 = (s32[4,2]{0,1:T(2,128)S(1)}, s32[4,2]{0,1:T(2,128)}, u32[]{:S(2)}) copy-start(s32[4,2]{0,1:T(2,128)} %param.11) | copy-start | bytes 100

commit v4 on v3

--- a/solution.py
+++ b/solution.py
@@ -14,17 +14,20 @@
 LEAD = 6
 SLOTS = 4
 OTHER_SLOTS = 8
+SEND_SLOTS = 16
 IN_FLIGHT = 4
 MESH = pl.DeviceIdType.MESH
 
 
 def exchange(
     dims,
-    coef_ref, x_ref, total_ref,
-    xo, xp, zin, pin, psend, bt, gsend, grecv, gz, gzt, gfin, gin, ffin,
-    xo_sem, xp_sem, ps_sem, pr_sem, zs_sem, zr_sem, gs_sem, gr_sem, fs_sem, fr_sem, ts_sem, tr_sem, ws_sem, wr_sem,
+    dom_ref, coef_hbm, x_ref, total_ref,
+    coef_ref, gacc, xo, xp, zin, pin, psend, bt, gsend, grecv, gz, gzt, gfin, gin, ffin,
+    coef_sem, xo_sem, xp_sem, ps_sem, pr_sem, zs_sem, zr_sem, gs_sem, gr_sem, fs_sem, fr_sem, ts_sem, tr_sem, ws_sem, wr_sem,
 ):
-    n_aux, n_orb, groups, per_group, row_groups = dims
+    n_aux, n_orb, groups, per_group, row_groups, parts = dims
+    part_chunks = per_group // parts
+    send_slots = psend.shape[0]
     chips = n_orb // 2
     half = per_group * CHUNK_ROWS
     chunks = groups * per_group
@@ -37,13 +40,6 @@
     following = jnp.where(core == 0, lax.rem(orb + 2, n_orb), lax.rem(orb + n_orb - 2, n_orb))
     last = stage == chips - 1
 
-    barrier = pltpu.get_barrier_semaphore()
-    for d in range(1, n_orb):
-        pl.semaphore_signal(barrier, inc=1, device_id=(aux, lax.rem(orb + d, n_orb)), device_id_type=MESH)
-    for d in range(1, n_aux):
-        pl.semaphore_signal(barrier, inc=1, device_id=(lax.rem(aux + d, n_aux), orb), device_id_type=MESH)
-    pl.semaphore_wait(barrier, n_orb - 1 + n_aux - 1)
-
     def load(t, base, buf, sem, slots):
         g, u = t // per_group, lax.rem(t, per_group)
         start = pl.multiple_of(base * half + u * CHUNK_ROWS, 16)
@@ -64,13 +60,13 @@
         parts = []
         for k in range(2):
             parts.append(
-                jnp.dot(buf[slot, k], coef_ref[g * 2 + k], preferred_element_type=jnp.float32)
+                jnp.dot(buf[slot, k], coef_ref[dom_ref[g * 2 + k]], preferred_element_type=jnp.float32)
             )
         return jnp.concatenate(parts, axis=1)
 
     def to_peer(t):
         return pltpu.make_async_remote_copy(
-            psend.at[t], pin.at[t], ps_sem.at[t], pr_sem.at[t], device_id=(aux, peer), device_id_type=MESH
+            psend.at[lax.rem(t, send_slots)], pin.at[t], ps_sem.at[lax.rem(t, send_slots)], pr_sem.at[t], device_id=(aux, peer), device_id_type=MESH
         )
 
     def to_next(t):
@@ -127,31 +123,43 @@
 
         lax.fori_loop(0, g + 1, body, 0)
 
-    def gram(g):
+    def gram(g, p):
         par = lax.rem(g, 2)
 
-        @pl.when(g >= 2)
+        @pl.when(jnp.logical_and(p == 0, g >= 2))
         def _():
             drain(g - 2)
 
-        first = g * per_group
+        first = g * per_group + p * part_chunks
 
         def column():
-            return zin[pl.ds(first, per_group)].reshape(half, GROUP)
+            return zin[pl.ds(first, part_chunks)].reshape(part_chunks * CHUNK_ROWS, GROUP)
 
         def block(r):
-            gsend[par, r] = jnp.dot(bt[r], column(), preferred_element_type=jnp.float32).astype(jnp.bfloat16)
-
-            @pl.when(line_of(native(r, g)) != aux)
-            def _():
-                to_reducer(par, r, g).start()
+            value = jnp.dot(bt[r, p], column(), preferred_element_type=jnp.float32)
+
+            @pl.when(p == 0)
+            def _():
+                gacc[r] = value
+
+            @pl.when(p > 0)
+            def _():
+                gacc[r] += value
+
+            @pl.when(p == parts - 1)
+            def _():
+                gsend[par, r] = gacc[r].astype(jnp.bfloat16)
+
+                @pl.when(line_of(native(r, g)) != aux)
+                def _():
+                    to_reducer(par, r, g).start()
 
         def body(r, carry):
             block(r)
             return carry
 
         lax.fori_loop(0, g, body, 0)
-        bt[g] = column().T
+        bt[g, p] = column().T
         block(g)
 
     def combine(g):
@@ -205,14 +213,35 @@
 
         lax.fori_loop(0, g + 1, body, 0)
 
+    coef_loads = [
+        pltpu.make_async_copy(coef_hbm.at[:, pl.ds(v * BS, BS)], coef_ref.at[v], coef_sem.at[v])
+        for v in range(coef_ref.shape[0])
+    ]
+    for copy in coef_loads:
+        copy.start()
     for t in range(OTHER_SLOTS):
         load_other(t).start()
     for t in range(SLOTS):
         load_own(t).start()
 
+    barrier = pltpu.get_barrier_semaphore()
+    for d in range(1, n_orb):
+        pl.semaphore_signal(barrier, inc=1, device_id=(aux, lax.rem(orb + d, n_orb)), device_id_type=MESH)
+    for d in range(1, n_aux):
+        pl.semaphore_signal(barrier, inc=1, device_id=(lax.rem(aux + d, n_aux), orb), device_id_type=MESH)
+    pl.semaphore_wait(barrier, n_orb - 1 + n_aux - 1)
+
+    for copy in coef_loads:
+        copy.wait()
+
     def help_peer(t):
         load_other(t).wait()
-        psend[t] = transform(t, xp, OTHER_SLOTS).astype(jnp.bfloat16)
+
+        @pl.when(t >= send_slots)
+        def _():
+            to_peer(t - send_slots).wait_send()
+
+        psend[lax.rem(t, send_slots)] = transform(t, xp, OTHER_SLOTS).astype(jnp.bfloat16)
         to_peer(t).start()
 
         @pl.when(t + OTHER_SLOTS < chunks)
@@ -266,9 +295,9 @@
         def _():
             combine(g - 1)
 
-        @pl.when(jnp.logical_and(last, lax.rem(now, per_group) == per_group - 1))
-        def _():
-            gram(g)
+        @pl.when(jnp.logical_and(last, lax.rem(now, part_chunks) == part_chunks - 1))
+        def _():
+            gram(g, lax.rem(now, per_group) // part_chunks)
 
         return carry
 
@@ -335,7 +364,7 @@
         to_peer(t).wait_send()
         return carry
 
-    lax.fori_loop(0, chunks, sent, 0)
+    lax.fori_loop(chunks - send_slots, chunks, sent, 0)
 
     @pl.when(jnp.logical_not(last))
     def _():
@@ -376,12 +405,6 @@
             return carry
 
         lax.fori_loop(0, groups, passed, 0)
-
-
-def pick(dom_ref, coef_ref, chosen_ref):
-    for i in range(chosen_ref.shape[0]):
-        first = pl.multiple_of(dom_ref[i] * BS, BS)
-        chosen_ref[i] = coef_ref[:, pl.ds(first, BS)]
 
 
 def pair_totals(integrals, coeffs, domains):
@@ -393,31 +416,30 @@
     chunks = groups * per_group
     row_groups = occupied // n_aux // 2
     assert groups == n_orb and half % CHUNK_ROWS == 0
-    dims = (n_aux, n_orb, groups, per_group, row_groups)
+    parts = next(n for n in (4, 2, 1) if per_group % n == 0)
+    vir_blocks = coeffs.shape[1] // BS
+    dims = (n_aux, n_orb, groups, per_group, row_groups, parts)
     bf16 = jnp.bfloat16
-    chosen = pl.pallas_call(
-        pick,
-        out_shape=jax.ShapeDtypeStruct((occupied, ao_local, BS), bf16),
-        in_specs=[pl.BlockSpec(memory_space=pltpu.SMEM), pl.BlockSpec(memory_space=pltpu.VMEM)],
-        out_specs=pl.BlockSpec(memory_space=pltpu.VMEM),
-    )(domains, coeffs)
     vmem = pltpu.VMEM
     dma = pltpu.SemaphoreType.DMA
     return pl.pallas_call(
         functools.partial(exchange, dims),
         out_shape=jax.ShapeDtypeStruct((row_groups, GROUP, GROUP), jnp.float32),
         in_specs=[
-            pl.BlockSpec(memory_space=pltpu.VMEM),
+            pl.BlockSpec(memory_space=pltpu.SMEM),
+            pl.BlockSpec(memory_space=pl.ANY),
             pl.BlockSpec(memory_space=pl.ANY),
         ],
         out_specs=pl.BlockSpec(memory_space=pltpu.VMEM),
         scratch_shapes=[
+            vmem((vir_blocks, ao_local, BS), bf16),
+            vmem((groups, GROUP, GROUP), jnp.float32),
             vmem((SLOTS, 2, CHUNK_ROWS, ao_local), bf16),
             vmem((OTHER_SLOTS, 2, CHUNK_ROWS, ao_local), bf16),
             vmem((chunks, CHUNK_ROWS, GROUP), bf16),
             vmem((chunks, CHUNK_ROWS, GROUP), bf16),
-            vmem((chunks, CHUNK_ROWS, GROUP), bf16),
-            vmem((groups, GROUP, half), bf16),
+            vmem((min(SEND_SLOTS, chunks), CHUNK_ROWS, GROUP), bf16),
+            vmem((groups, parts, GROUP, half // parts), bf16),
             vmem((2, groups, GROUP, GROUP), bf16),
             vmem((n_aux - 1, row_groups, groups, GROUP, GROUP), bf16),
             vmem((row_groups, groups, GROUP, GROUP), bf16),
@@ -425,9 +447,10 @@
             vmem((2, row_groups, GROUP, GROUP), bf16),
             vmem((2, groups, GROUP, GROUP), bf16),
             vmem((row_groups, GROUP, GROUP), bf16),
+            dma((vir_blocks,)),
             dma((SLOTS,)),
             dma((OTHER_SLOTS,)),
-            dma((chunks,)),
+            dma((min(SEND_SLOTS, chunks),)),
             dma((chunks,)),
             dma((chunks,)),
             dma((chunks,)),
@@ -441,12 +464,12 @@
             dma((row_groups,)),
         ],
         compiler_params=pltpu.CompilerParams(
-            collective_id=0, has_side_effects=True, vmem_limit_bytes=62 * 1024 * 1024
+            collective_id=0, has_side_effects=True, vmem_limit_bytes=63 * 1024 * 1024
         ),
         cost_estimate=pl.CostEstimate(
             flops=2 * occupied * aux_rows * ao_local * BS, bytes_accessed=2 * integrals.size, transcendentals=0
         ),
-    )(chosen, integrals)
+    )(domains, coeffs, integrals)
 
 
 def shards(integrals, coeffs, domains, eps_occ, eps_vir, pair_mask):

time: 151 us -> 150 us (level)
    pallas_call x1 -> x0, Pallas kernels: 2.49 us -> none  [pair_totals(): pl.pallas_call(pick, out_shape=jax.ShapeDtypeStruct((occupied, ao_local,...]
where the time goes in v4:
time: 150 us; the launch traced here: 149 us
  Pallas kernels  145 us (97%)
  local copies, waits for them, and re-layouts  2.24 us (1%)
  other arithmetic  1.65 us (1%)
    pallas_call x1, Pallas kernels, pair_totals(): pl.pallas_call(functools.partial(exchange, dims), out_shape=jax.ShapeDtyp...  145 us

profile of v4, /device:TPU:23, one launch (start us, length us, event | category | flops | bytes accessed | tf_op | source)
XLA Modules:
  0.0 149.3 jit_solution(7672186271241257335)
XLA Ops:
  0.6 0.0 copy-start
  0.6 0.0 copy-start.2
  0.7 0.0 copy-start.3
  0.7 0.0 copy-start.1
  0.7 144.5 %shard_map.77 = f32[2,256,256]{2,1,0:T(8,128)} custom-call(s32[16]{0:T(128)} %dom_ref.1, bf16[256,2048]{1,0:T(8,128)(2,1)} %coef_hbm.1, bf16[16,3840,256]{2,1,0:T(8,128)(2,1)} %x_ref.1), custom_call_target="tpu_custom_call" | custom-call | flops 4026531840 | bytes 31457280 | tf_op jit(solution)/shard_map/pallas_call | solution.py:425
  145.2 1.3 reshape.16
  146.5 0.0 copy-done.3
  146.5 0.1 dynamic_slice.15
  146.6 0.1 dynamic_slice.14
  146.7 0.0 copy-done
  146.7 0.0 copy-done.2
  146.7 0.2 fusion
  146.9 0.0 copy-done.1
  146.9 0.1 copy.9
  147.0 1.6 %multiply_reduce_fusion = (f32[4,2]{1,0:T(4,128)S(1)}, bf16[4,128,2,128]{3,2,1,0:T(2,128)(2,1)}) fusion(f32[4,128,2,128]{3,2,1,0:T(2,128)S(1)} %reshape.16, f32[2]{0:T(128)S(1)} %dynamic_slice.15, f32[4]{0:T(128)S(1)} %dynamic_slice.14, f32[2,128]{1,0:T(2,128)S(1)} %constant_dynamic-slice_fusion, f32[4,128]{1,0:T(4,128)S(1)} %constant_dynamic-slice_fusion.1, ...), kind=kLoop, calls=%fused_computation | loop fusion | flops 1179640 | bytes 789592 | tf_op jit(solution)/shard_map/reduce_sum | solution.py:502
  148.7 0.7 copy.10
  (4 shorter events, 0.0 us)
Async XLA Ops:
  0.6 146.1 %copy-start = (f32[2048]{0:T(1024)S(1)}, f32[2048]{0:T(1024)}, u32[]{:S(2)}) copy-start(f32[2048]{0:T(1024)} %param.10) | copy-start | bytes 24580
  0.6 146.1 %copy-start.2 = (s32[16]{0:T(128)S(1)}, s32[16]{0:T(128)}, u32[]{:S(2)}) copy-start(s32[16]{0:T(128)} %dom_ref.1) | copy-start | bytes 196
  0.7 145.9 %copy-start.3 = (f32[16]{0:T(128)S(1)}, f32[16]{0:T(128)}, u32[]{:S(2)}) copy-start(f32[16]{0:T(128)} %param.9) | copy-start | bytes 196
  0.7 146.3 %copy-start.1 = (s32[4,2]{0,1:T(2,128)S(1)}, s32[4,2]{0,1:T(2,128)}, u32[]{:S(2)}) copy-start(s32[4,2]{0,1:T(2,128)} %param.11) | copy-start | bytes 100

commit v5 on v4

--- a/solution.py
+++ b/solution.py
@@ -181,15 +181,6 @@
                     acc += grecv[d - 1, rl, m].astype(jnp.float32)
 
                 def deliver(straight, turned):
-                    @pl.when(m == orb)
-                    def _():
-                        gfin[core, rl] = straight().astype(jnp.bfloat16)
-
-                    @pl.when(m != orb)
-                    def _():
-                        gz[rl, m] = straight().astype(jnp.bfloat16)
-                        to_owner(rl, m).start()
-
                     @pl.when(m != n)
                     def _():
                         @pl.when(n == orb)
@@ -200,6 +191,15 @@
                         def _():
                             gzt[rl, m] = turned().astype(jnp.bfloat16)
                             to_forwarder(rl, m, n).start()
+
+                    @pl.when(m == orb)
+                    def _():
+                        gfin[core, rl] = straight().astype(jnp.bfloat16)
+
+                    @pl.when(m != orb)
+                    def _():
+                        gz[rl, m] = straight().astype(jnp.bfloat16)
+                        to_owner(rl, m).start()
 
                 @pl.when(n == r)
                 def _():

time: 150 us -> 149 us (level)
  no operation moved by 1% of the time
where the time goes in v5:
time: 149 us
  Pallas kernels  144 us (97%)
  local copies, waits for them, and re-layouts  2.24 us (2%)
  other arithmetic  1.65 us (1%)
    pallas_call x1, Pallas kernels, pair_totals(): pl.pallas_call(functools.partial(exchange, dims), out_shape=jax.ShapeDtyp...  144 us

profile of v5, /device:TPU:23, one launch (start us, length us, event | category | flops | bytes accessed | tf_op | source)
XLA Modules:
  0.0 149.1 jit_solution(12206121592532542558)
XLA Ops:
  0.6 0.0 copy-start
  0.6 0.0 copy-start.2
  0.7 0.0 copy-start.3
  0.7 0.0 copy-start.1
  0.7 144.3 %shard_map.77 = f32[2,256,256]{2,1,0:T(8,128)} custom-call(s32[16]{0:T(128)} %dom_ref.1, bf16[256,2048]{1,0:T(8,128)(2,1)} %coef_hbm.1, bf16[16,3840,256]{2,1,0:T(8,128)(2,1)} %x_ref.1), custom_call_target="tpu_custom_call" | custom-call | flops 4026531840 | bytes 31457280 | tf_op jit(solution)/shard_map/pallas_call | solution.py:425
  145.0 1.3 reshape.16
  146.3 0.0 copy-done.3
  146.3 0.1 dynamic_slice.15
  146.4 0.1 dynamic_slice.14
  146.4 0.0 copy-done
  146.4 0.0 copy-done.2
  146.5 0.2 fusion
  146.7 0.0 copy-done.1
  146.7 0.1 copy.9
  146.8 1.6 %multiply_reduce_fusion = (f32[4,2]{1,0:T(4,128)S(1)}, bf16[4,128,2,128]{3,2,1,0:T(2,128)(2,1)}) fusion(f32[4,128,2,128]{3,2,1,0:T(2,128)S(1)} %reshape.16, f32[2]{0:T(128)S(1)} %dynamic_slice.15, f32[4]{0:T(128)S(1)} %dynamic_slice.14, f32[2,128]{1,0:T(2,128)S(1)} %constant_dynamic-slice_fusion, f32[4,128]{1,0:T(4,128)S(1)} %constant_dynamic-slice_fusion.1, ...), kind=kLoop, calls=%fused_computation | loop fusion | flops 1179640 | bytes 789592 | tf_op jit(solution)/shard_map/reduce_sum | solution.py:502
  148.4 0.7 copy.10
  (4 shorter events, 0.0 us)
Async XLA Ops:
  0.6 145.8 %copy-start = (f32[2048]{0:T(1024)S(1)}, f32[2048]{0:T(1024)}, u32[]{:S(2)}) copy-start(f32[2048]{0:T(1024)} %param.10) | copy-start | bytes 24580
  0.6 145.8 %copy-start.2 = (s32[16]{0:T(128)S(1)}, s32[16]{0:T(128)}, u32[]{:S(2)}) copy-start(s32[16]{0:T(128)} %dom_ref.1) | copy-start | bytes 196
  0.7 145.6 %copy-start.3 = (f32[16]{0:T(128)S(1)}, f32[16]{0:T(128)}, u32[]{:S(2)}) copy-start(f32[16]{0:T(128)} %param.9) | copy-start | bytes 196
  0.7 146.0 %copy-start.1 = (s32[4,2]{0,1:T(2,128)S(1)}, s32[4,2]{0,1:T(2,128)}, u32[]{:S(2)}) copy-start(s32[4,2]{0,1:T(2,128)} %param.11) | copy-start | bytes 100
